TPU v7x, 512 devices: a whole 4x4x16 slice. The times are simulated.
512 devices in a mesh: row: 32 (over z_lo, y), col: 16 (over z_hi, x, core).
Axes of the slice: x: 4, y: 4, z: 16 (z_hi: 2, z_lo: 8; z = z_hi * 8 + z_lo), core: 2. Of those that a mesh axis runs over, the one named last changes fastest.
Arguments:
- entries: int32 [128, 64, 128, 128], P('row', 'col'), may hold values from -2 to 2
- tile_cols: int32 [128, 64], P('row', 'col'), may hold values from 0 to 31
- block_now: int32 [32, 65536], P(None, ('col', 'row')), may hold values from 0 to 65520
- block_prev: int32 [32, 65536], P(None, ('col', 'row')), may hold values from 0 to 65520
- block_prev2: int32 [32, 65536], P(None, ('col', 'row')), may hold values from 0 to 65520
- gram_prev: int32 [32, 32], replicated, may hold values from 0 to 65520
- square_prev: int32 [32, 32], replicated, may hold values from 0 to 65520
- inverse_prev: int32 [32, 32], replicated, may hold values from 0 to 65520
- inverse_prev2: int32 [32, 32], replicated, may hold values from 0 to 65520
Outputs:
- next_block: float32 [32, 65536], P(None, ('col', 'row'))
- later_block: float32 [32, 65536], P(None, ('col', 'row'))
Inputs may be any that keep to these rules, and one draw needn't show every extreme that they name: `tile_cols`: stored tiles that name the same tile column in one tile row add. `block_prev`: residues. `block_prev2`: residues. `gram_prev`: residues. `square_prev`: residues. `inverse_prev`: residues. `inverse_prev2`: residues.
All inputs are finite; a program needn't handle non-finite values.
Results may differ from a plain program's by a relative error of at most 0.0003.
Values sent between devices are 32-bit elements; how exact they have to be, the bound alone decides.
No kernel may reach another device: no remote copies, remote signals or barrier semaphores. Data moves between devices by JAX's collectives and lax.ppermute only.
A program may use at most 64 MiB of HBM per device.

v0:
```python
import jax
import jax.numpy as jnp
from jax import lax
from jax.sharding import PartitionSpec as P

modulus = 65521.0


def residue(values):
    return jnp.mod(values, modulus)


def split_digits(values):
    top_part = jnp.floor(values / 256.0)
    return (top_part, values - top_part * 256.0)


def fold_digits(top_sum, low_sum):
    return residue(residue(residue(top_sum) * 256.0) + residue(low_sum))


def fold_three(upper_part, middle, lower_part):
    return residue(
        residue(residue(upper_part) * 15.0) + residue(residue(middle) * 256.0) + residue(lower_part)
    )


def mulmod(left_side, right_side):
    top_part, low_part = split_digits(right_side)
    return fold_digits(left_side * top_part, left_side * low_part)


def exact_dot(left_side, right_side):
    return jnp.dot(
        left_side, right_side, precision=lax.Precision.HIGHEST, preferred_element_type=jnp.float32
    )


def small_product(left_side, right_side):
    left_top, left_low = split_digits(left_side)
    right_top, right_low = split_digits(right_side)
    return fold_three(
        exact_dot(left_top, right_top),
        exact_dot(left_top, right_low) + exact_dot(left_low, right_top),
        exact_dot(left_low, right_low),
    )


def inverse_scalar(number):
    result = jnp.ones_like(number)
    square = number
    exponent = 65519
    for position in range(16):
        if exponent >> position & 1:
            result = mulmod(result, square)
        square = mulmod(square, square)
    return result


def inverse_matrix(matrix):
    matrix_order = matrix.shape[0]
    augmented = jnp.concatenate([matrix, jnp.eye(matrix_order, dtype=matrix.dtype)], axis=1)
    row_numbers = jnp.arange(matrix_order, dtype=jnp.int32)

    def eliminate(column, augmented):
        column = jnp.asarray(column).astype(jnp.int32)
        pivot_column = augmented[:, column]
        usable = (pivot_column != 0.0) & (row_numbers >= column)
        pivot_row_id = jnp.where(jnp.any(usable), jnp.argmax(usable), column)
        pivot_row = augmented[pivot_row_id]
        current_row = augmented[column]
        swapped = jnp.where(
            (row_numbers == column)[:, None],
            pivot_row[None, :],
            jnp.where((row_numbers == pivot_row_id)[:, None], current_row[None, :], augmented),
        )
        scaled = mulmod(pivot_row, inverse_scalar(pivot_row[column]))
        factors = jnp.where(row_numbers == column, 0.0, swapped[:, column])
        reduced = residue(swapped - mulmod(factors[:, None], scaled[None, :]) + modulus)
        return jnp.where((row_numbers == column)[:, None], scaled[None, :], reduced)

    augmented = lax.fori_loop(0, matrix_order, eliminate, augmented)
    return augmented[:, matrix_order:]


def coefficients(
    gram_now, square_now, inverse_now, inverse_prev, inverse_prev2, gram_old, square_old
):
    identity = jnp.eye(gram_now.shape[0], dtype=gram_now.dtype)
    first = residue(identity - small_product(residue(square_now + gram_now), inverse_now) + modulus)
    second = residue(modulus - small_product(gram_now, inverse_prev))
    middle = residue(identity - small_product(inverse_prev, gram_old) + modulus)
    third = residue(
        modulus
        - small_product(small_product(residue(square_old + gram_old), middle), inverse_prev2)
    )
    return jnp.concatenate([first, second, third], axis=1)


def digit_stack(values):
    top_part, low_part = split_digits(values)
    return jnp.stack([top_part, low_part]).astype(jnp.bfloat16)


def combine_blocks(coeffs, stacked):
    products = jnp.einsum(
        "dab,ebn->dean",
        digit_stack(coeffs),
        digit_stack(stacked),
        preferred_element_type=jnp.float32,
    )
    return fold_three(products[0, 0], products[0, 1] + products[1, 0], products[1, 1])


def gram_local(first, second):
    column_count = first.shape[1]
    group_width = min(column_count, 128)
    groups = column_count // group_width
    first_digits = digit_stack(first).reshape(2, first.shape[0], groups, group_width)
    second_digits = digit_stack(second).reshape(2, second.shape[0], groups, group_width)
    products = jnp.einsum(
        "dagw,ecgw->gdeac", first_digits, second_digits, preferred_element_type=jnp.float32
    )
    per_group = fold_three(
        products[:, 0, 0], products[:, 0, 1] + products[:, 1, 0], products[:, 1, 1]
    )
    return residue(jnp.sum(per_group, axis=0))


def digit_pair(values):
    top_part, low_part = split_digits(values)
    return jnp.stack([top_part, low_part])


def forward_partial(block_full, tile_values, tile_cols):
    tile_rows, slot_count, tile_size = (
        tile_values.shape[0],
        tile_values.shape[1],
        tile_values.shape[2],
    )
    block_rows = block_full.shape[0]
    top_part, low_part = split_digits(block_full)
    digits = jnp.concatenate([top_part, low_part], axis=0).astype(jnp.bfloat16)
    digits = digits.reshape(2 * block_rows, -1, tile_size)
    picked = jnp.take(digits, tile_cols.reshape(-1), axis=1).reshape(
        2 * block_rows, tile_rows, slot_count, tile_size
    )
    raw_sums = jnp.einsum("brsk,rsjk->brj", picked, tile_values, preferred_element_type=jnp.float32)
    return fold_digits(raw_sums[:block_rows], raw_sums[block_rows:]).reshape(
        block_rows, tile_rows * tile_size
    )


def backward_partial(projected, tile_values, onehot):
    tile_rows, tile_size = (tile_values.shape[0], tile_values.shape[2])
    block_rows = projected.shape[0]
    top_part, low_part = split_digits(projected)
    digits = (
        jnp.concatenate([top_part, low_part], axis=0)
        .astype(jnp.bfloat16)
        .reshape(2 * block_rows, tile_rows, tile_size)
    )
    spread = jnp.einsum("brj,rsjk->brsk", digits, tile_values, preferred_element_type=jnp.float32)
    raw_sums = jnp.einsum(
        "brsk,rsc->bck",
        spread,
        onehot,
        precision=lax.Precision.HIGHEST,
        preferred_element_type=jnp.float32,
    )
    return fold_digits(raw_sums[:block_rows], raw_sums[block_rows:]).reshape(block_rows, -1)


def body(
    entries,
    tile_cols,
    block_now,
    block_prev,
    block_prev2,
    gram_prev,
    square_prev,
    inverse_prev,
    inverse_prev2,
):
    tile_values = entries.astype(jnp.bfloat16)
    tile_size = tile_values.shape[2]
    share_width = block_now.shape[1]
    col_tiles = share_width * lax.axis_size("row") // tile_size
    onehot = (
        tile_cols[:, :, None] == jnp.arange(col_tiles, dtype=jnp.int32)[None, None, :]
    ).astype(jnp.float32)
    current = block_now.astype(jnp.float32)
    earlier = block_prev.astype(jnp.float32)
    earliest = block_prev2.astype(jnp.float32)
    gram_old = gram_prev.astype(jnp.float32)
    square_old = square_prev.astype(jnp.float32)
    inverse_old = inverse_prev.astype(jnp.float32)
    inverse_older = inverse_prev2.astype(jnp.float32)
    results = []
    for iteration in range(2):
        block_full = lax.all_gather(current, "row", axis=1, tiled=True)
        projected = residue(lax.psum(forward_partial(block_full, tile_values, tile_cols), "col"))
        partial_term = backward_partial(projected, tile_values, onehot)
        applied = residue(lax.psum_scatter(partial_term, "row", scatter_dimension=1, tiled=True))
        current_own = current
        both_sums = lax.psum(
            jnp.stack(
                [
                    digit_pair(gram_local(current_own, applied)),
                    digit_pair(gram_local(applied, applied)),
                ]
            ),
            ("row", "col"),
        )
        gram_now = fold_digits(both_sums[0, 0], both_sums[0, 1])
        square_now = fold_digits(both_sums[1, 0], both_sums[1, 1])
        inverse_now = inverse_matrix(gram_now)
        coeffs = coefficients(
            gram_now, square_now, inverse_now, inverse_old, inverse_older, gram_old, square_old
        )
        stacked = jnp.concatenate([current, earlier, earliest], axis=0)
        following = residue(applied + combine_blocks(coeffs, stacked))
        results.append(following / modulus)
        earliest, earlier, current = (earlier, current, following)
        inverse_older, inverse_old = (inverse_old, inverse_now)
        gram_old, square_old = (gram_now, square_now)
    return (results[0], results[1])


def solution(mesh):
    placed = (
        P("row", "col", None, None),
        P("row", "col"),
        P(None, ("col", "row")),
        P(None, ("col", "row")),
        P(None, ("col", "row")),
        P(),
        P(),
        P(),
        P(),
    )
    return jax.shard_map(
        body,
        mesh=mesh,
        in_specs=placed,
        out_specs=(P(None, ("col", "row")), P(None, ("col", "row"))),
        check_vma=False,
    )
```

profile of v0, /device:TPU:1, one launch (start us, length us, event | category | flops | bytes accessed | tf_op | source)
XLA Modules:
  0.0 2244.6 jit_solution(948067549384732013)
XLA Ops:
  7.2 0.8 reshape.1652
  8.8 114.7 %all_gather.6 = f32[32,4096]{1,0:T(8,128)S(1)} all-gather(f32[32,128]{1,0:T(8,128)S(1)} %get-tuple-element.319), channel_id=1, replica_groups=mesh['row'=32,'col'=16] {'row'}, dimensions={1}, use_global_device_ids=true | all-gather | bytes 540672 | tf_op jit(solution)/shard_map/all_gather | solution.py:201
  124.9 0.8 copy_bitcast_fusion.7
  129.3 247.2 %all-reduce.3.cloned.1.call-done = f32[32,512]{1,0:T(8,128)} async-done(((f32[32,512]{1,0:T(8,128)}), f32[32,512]{1,0:T(8,128)}) %all-reduce.3.cloned.1.call-update) | async-done | bytes 65552 | tf_op jit(solution)/shard_map/psum | solution.py:202
  376.5 0.9 fusion.102
  378.1 1.1 convolution_bitcast_fusion.1
  379.2 1.1 add_select_fusion.22
  380.3 1.1 copy.355
  383.5 212.7 %reduce-scatter.3.cloned.1.call-done = f32[32,128]{1,0:T(8,128)} async-done(((f32[32,4096]{1,0:T(8,128)}), f32[32,128]{1,0:T(8,128)}) %reduce-scatter.3.cloned.1.call-update) | async-done | bytes 16400 | tf_op jit(solution)/shard_map/reduce_scatter | solution.py:204
  596.2 0.7 fusion.339
  597.5 125.4 %psum.29 = f32[2,2,32,32]{2,3,1,0:T(8,128)S(1)} all-reduce(f32[2,2,32,32]{2,3,1,0:T(8,128)S(1)} %pad_maximum_fusion.2), channel_id=1, replica_groups=mesh['row'=32,'col'=16] {'row','col'}, use_global_device_ids=true, to_apply=%region_2.4 | all-reduce | flops 4096 | bytes 32768 | tf_op jit(solution)/shard_map/psum | solution.py:206
  722.9 403.5 %while.36 = (s32[]{:T(128)}, f32[32,64]{0,1:T(8,128)S(1)}, s32[]{:T(128)}, s32[]{:T(128)}, s32[]{:T(128)}, /*index=5*/s32[]{:T(128)}, s32[]{:T(128)}, f32[]{:T(128)}, f32[]{:T(128)}, f32[]{:T(128)}, /*index=10*/f32[]{:T(128)}) while((s32[]{:T(128)}, f32[32,64]{0,1:T(8,128)S(1)}, s32[]{:T(128)}, s32[]{:T(128)}, ...), condition=%wide.region_6.8_spmd.clone.clone, body=%wide.region_3.7_spmd.clone.clone.sunk | while | flops 87498 | bytes 50118 | solution.py:82
  723.6 0.7 iota_reduce_fusion.4
  736.2 0.7 iota_reduce_fusion.4
  761.4 0.7 iota_reduce_fusion.4
  799.3 0.7 iota_reduce_fusion.4
  837.1 0.7 iota_reduce_fusion.4
  862.3 0.7 iota_reduce_fusion.4
  874.9 0.7 iota_reduce_fusion.4
  900.1 0.7 iota_reduce_fusion.4
  938.0 0.7 iota_reduce_fusion.4
  1129.8 103.1 %all_gather.7 = f32[32,4096]{1,0:T(8,128)S(1)} all-gather(f32[32,128]{1,0:T(8,128)S(1)} %get-tuple-element.280), channel_id=1, replica_groups=mesh['row'=32,'col'=16] {'row'}, dimensions={1}, use_global_device_ids=true | all-gather | bytes 540672 | tf_op jit(solution)/shard_map/all_gather | solution.py:201
  1234.2 0.8 copy_bitcast_fusion.6
  1235.6 249.9 %all-reduce.5.cloned.1.call-done = f32[32,512]{1,0:T(8,128)} async-done(((f32[32,512]{1,0:T(8,128)}), f32[32,512]{1,0:T(8,128)}) %all-reduce.5.cloned.1.call-update) | async-done | bytes 65552 | tf_op jit(solution)/shard_map/psum | solution.py:202
  1485.5 0.9 fusion.103
  1486.7 1.1 convolution_bitcast_fusion
  1487.7 1.1 add_select_fusion.18
  1488.9 1.1 copy.354
  1491.4 213.1 %reduce-scatter.5.cloned.1.call-done = f32[32,128]{1,0:T(8,128)} async-done(((f32[32,4096]{1,0:T(8,128)}), f32[32,128]{1,0:T(8,128)}) %reduce-scatter.5.cloned.1.call-update) | async-done | bytes 16400 | tf_op jit(solution)/shard_map/reduce_scatter | solution.py:204
  1704.5 0.7 fusion.343
  1705.8 125.7 %psum.31 = f32[2,2,32,32]{2,3,1,0:T(8,128)S(1)} all-reduce(f32[2,2,32,32]{2,3,1,0:T(8,128)S(1)} %pad_maximum_fusion.3), channel_id=1, replica_groups=mesh['row'=32,'col'=16] {'row','col'}, use_global_device_ids=true, to_apply=%region_9.11 | all-reduce | flops 4096 | bytes 32768 | tf_op jit(solution)/shard_map/psum | solution.py:206
  1831.6 403.5 %while.37 = (s32[]{:T(128)}, f32[32,64]{0,1:T(8,128)S(1)}, s32[]{:T(128)}, s32[]{:T(128)}, s32[]{:T(128)}, /*index=5*/s32[]{:T(128)}, s32[]{:T(128)}, f32[]{:T(128)}, f32[]{:T(128)}, f32[]{:T(128)}, /*index=10*/f32[]{:T(128)}) while((s32[]{:T(128)}, f32[32,64]{0,1:T(8,128)S(1)}, s32[]{:T(128)}, s32[]{:T(128)}, ...), condition=%wide.region_13.15_spmd.clone.clone, body=%wide.region_10.14_spmd.clone.clone.sunk | while | flops 87498 | bytes 50118 | solution.py:82
  (706 shorter events, 178.9 us)
Async XLA Ops:
  7.2 116.5 %copy-start = (s32[4,4,128,128]{3,2,1,0:T(8,128)S(1)}, s32[4,4,128,128]{3,2,1,0:T(8,128)}, u32[]{:S(2)}) copy-start(s32[4,4,128,128]{3,2,1,0:T(8,128)} %param.15) | copy-start | bytes 3145732
  7.2 369.3 %all-reduce.3.cloned.1.call-start = ((), (), s32[]{:S(2)}) async-start(), calls=%async_computation.2 | async-start | bytes 131072 | tf_op jit(solution)/shard_map/psum | solution.py:202
  125.7 0.7 copy-start.5
  125.7 0.8 copy-start.6
  125.7 470.4 %reduce-scatter.3.cloned.1.call-start = ((), (), s32[]{:S(2)}) async-start(), calls=%async_computation.3 | async-start | bytes 540672 | tf_op jit(solution)/shard_map/reduce_scatter | solution.py:204
  126.9 0.7 copy-start.7
  128.2 0.7 copy-start.8
  377.4 0.7 copy-start.4
  381.5 1104.0 %all-reduce.5.cloned.1.call-start = ((), (), s32[]{:S(2)}) async-start(), calls=%async_computation.4 | async-start | bytes 131072 | tf_op jit(solution)/shard_map/psum | solution.py:202
  382.0 0.7 copy-start.9
  382.0 0.7 copy-start.10
  382.8 0.7 copy-start.1
  1129.0 0.7 copy-start.2
  1235.0 469.5 %reduce-scatter.5.cloned.1.call-start = ((), (), s32[]{:S(2)}) async-start(), calls=%async_computation.5 | async-start | bytes 540672 | tf_op jit(solution)/shard_map/reduce_scatter | solution.py:204
  2236.6 0.7 copy-start.3
Sparse Core Ops, SparseCore 0:
  125.8 250.6 all-reduce.2
  381.6 214.5 reduce-scatter.2
  1235.1 250.3 all-reduce.4
  1490.1 214.3 reduce-scatter.4
where the time goes:
time: 2250 us; the launch traced here: 2240 us
  waiting for transfers between devices  923 us (41%)
  loops' own time  641 us (28%)
  blocking collectives  469 us (21%)
  other arithmetic  139 us (6%)
  local copies, waits for them, and re-layouts  47.5 us (2%)
    another operation x2, loops' own time, inverse_matrix(): augmented = lax.fori_loop(0, matrix_order, eliminate, augmented)  641 us
    psum x2, waiting for transfers between devices, body(): lax.psum(forward_partial(block_full, tile_values, tile_cols), 'col')  497 us
    reduce_scatter x2, waiting for transfers between devices, body(): lax.psum_scatter(partial_term, 'row', scatter_dimension=1, tiled=True)  426 us
    psum x2, blocking collectives, body(): lax.psum(jnp.stack([digit_pair(gram_local(current_own, applied)), digit_p...  251 us
    all_gather x2, blocking collectives, body(): block_full = lax.all_gather(current, 'row', axis=1, tiled=True)  218 us
    another operation x64, other arithmetic, eliminate(): pivot_row_id = jnp.where(jnp.any(usable), jnp.argmax(usable), column)  46.5 us
  transfers between devices with their start and end apart: 4, of which 4 were waited for; matrix products, arithmetic and copies ran while one was open for 0% of the time, Pallas kernels for 0%

commit v1 on v0

--- a/solution.py
+++ b/solution.py
@@ -203,15 +203,11 @@
         partial_term = backward_partial(projected, tile_values, onehot)
         applied = residue(lax.psum_scatter(partial_term, "row", scatter_dimension=1, tiled=True))
         current_own = current
-        both_sums = lax.psum(
-            jnp.stack(
-                [
-                    digit_pair(gram_local(current_own, applied)),
-                    digit_pair(gram_local(applied, applied)),
-                ]
-            ),
-            ("row", "col"),
+        both_sums = jnp.stack(
+            [digit_pair(gram_local(current_own, applied)), digit_pair(gram_local(applied, applied))]
         )
+        for c in ("col", "row"):
+            both_sums = lax.psum(both_sums, c)
         gram_now = fold_digits(both_sums[0, 0], both_sums[0, 1])
         square_now = fold_digits(both_sums[1, 0], both_sums[1, 1])
         inverse_now = inverse_matrix(gram_now)

time: 2250 us -> 2740 us (1.22); the launches traced: 2240 us -> 2700 us
  blocking collectives: 469 us -> 880 us
  waiting for transfers between devices: 923 us -> 967 us
    psum x2 -> x4, blocking collectives: 251 us -> 665 us  [body(): both_sums = lax.psum(both_sums, c)]
    psum x2, waiting for transfers between devices: 497 us -> 541 us  [body(): lax.psum(forward_partial(block_full, tile_values, tile_cols), 'col')]
where the time goes in v1:
time: 2740 us; the launch traced here: 2700 us
  waiting for transfers between devices  967 us (35%)
  blocking collectives  880 us (32%)
  loops' own time  641 us (23%)
  other arithmetic  139 us (5%)
  local copies, waits for them, and re-layouts  47.5 us (2%)
    psum x4, blocking collectives, body(): both_sums = lax.psum(both_sums, c)  665 us
    another operation x2, loops' own time, inverse_matrix(): augmented = lax.fori_loop(0, matrix_order, eliminate, augmented)  641 us
    psum x2, waiting for transfers between devices, body(): lax.psum(forward_partial(block_full, tile_values, tile_cols), 'col')  541 us
    reduce_scatter x2, waiting for transfers between devices, body(): lax.psum_scatter(partial_term, 'row', scatter_dimension=1, tiled=True)  426 us
    all_gather x2, blocking collectives, body(): block_full = lax.all_gather(current, 'row', axis=1, tiled=True)  215 us
  transfers between devices with their start and end apart: 4, of which 4 were waited for; matrix products, arithmetic and copies ran while one was open for 0% of the time, Pallas kernels for 0%

profile of v1, /device:TPU:1, one launch (start us, length us, event | category | flops | bytes accessed | tf_op | source)
XLA Modules:
  0.0 2699.5 jit_solution(183661386175523601)
XLA Ops:
  7.2 0.8 reshape.1652
  8.8 114.7 %all_gather.6 = f32[32,4096]{1,0:T(8,128)S(1)} all-gather(f32[32,128]{1,0:T(8,128)S(1)} %get-tuple-element.319), channel_id=1, replica_groups=mesh['row'=32,'col'=16] {'row'}, dimensions={1}, use_global_device_ids=true | all-gather | bytes 540672 | tf_op jit(solution)/shard_map/all_gather | solution.py:201
  124.9 0.8 copy_bitcast_fusion.7
  129.3 247.2 %all-reduce.3.cloned.1.call-done = f32[32,512]{1,0:T(8,128)} async-done(((f32[32,512]{1,0:T(8,128)}), f32[32,512]{1,0:T(8,128)}) %all-reduce.3.cloned.1.call-update) | async-done | bytes 65552 | tf_op jit(solution)/shard_map/psum | solution.py:202
  376.5 0.9 fusion.102
  378.1 1.1 convolution_bitcast_fusion.1
  379.2 1.1 add_select_fusion.22
  380.3 1.1 copy.355
  383.5 212.7 %reduce-scatter.3.cloned.1.call-done = f32[32,128]{1,0:T(8,128)} async-done(((f32[32,4096]{1,0:T(8,128)}), f32[32,128]{1,0:T(8,128)}) %reduce-scatter.3.cloned.1.call-update) | async-done | bytes 16400 | tf_op jit(solution)/shard_map/reduce_scatter | solution.py:204
  596.2 0.7 fusion.339
  597.5 135.6 %psum.43 = f32[2,2,32,32]{2,3,1,0:T(8,128)S(1)} all-reduce(f32[2,2,32,32]{2,3,1,0:T(8,128)S(1)} %pad_maximum_fusion.2), channel_id=1, replica_groups=mesh['row'=32,'col'=16] {'col'}, use_global_device_ids=true, to_apply=%region_2.4 | all-reduce | flops 4096 | bytes 32768 | tf_op jit(solution)/shard_map/psum | solution.py:210
  733.1 197.0 %psum.44 = f32[2,2,32,32]{2,3,1,0:T(8,128)S(1)} all-reduce(f32[2,2,32,32]{2,3,1,0:T(8,128)S(1)} %psum.43), channel_id=1, replica_groups=mesh['row'=32,'col'=16] {'row'}, use_global_device_ids=true, to_apply=%region_3.5 | all-reduce | flops 4096 | bytes 32768 | tf_op jit(solution)/shard_map/psum | solution.py:210
  930.2 403.5 %while.36 = (s32[]{:T(128)}, f32[32,64]{0,1:T(8,128)S(1)}, s32[]{:T(128)}, s32[]{:T(128)}, s32[]{:T(128)}, /*index=5*/s32[]{:T(128)}, s32[]{:T(128)}, f32[]{:T(128)}, f32[]{:T(128)}, f32[]{:T(128)}, /*index=10*/f32[]{:T(128)}) while((s32[]{:T(128)}, f32[32,64]{0,1:T(8,128)S(1)}, s32[]{:T(128)}, s32[]{:T(128)}, ...), condition=%wide.region_7.9_spmd.clone.clone, body=%wide.region_4.8_spmd.clone.clone.sunk | while | flops 87498 | bytes 50118 | solution.py:82
  956.1 0.7 iota_reduce_fusion.4
  968.7 0.7 iota_reduce_fusion.4
  981.3 0.7 iota_reduce_fusion.4
  993.9 0.7 iota_reduce_fusion.4
  1006.5 0.7 iota_reduce_fusion.4
  1019.1 0.7 iota_reduce_fusion.4
  1031.7 0.7 iota_reduce_fusion.4
  1337.0 100.1 %all_gather.7 = f32[32,4096]{1,0:T(8,128)S(1)} all-gather(f32[32,128]{1,0:T(8,128)S(1)} %get-tuple-element.280), channel_id=1, replica_groups=mesh['row'=32,'col'=16] {'row'}, dimensions={1}, use_global_device_ids=true | all-gather | bytes 540672 | tf_op jit(solution)/shard_map/all_gather | solution.py:201
  1438.4 0.8 copy_bitcast_fusion.6
  1439.8 293.5 %all-reduce.5.cloned.1.call-done = f32[32,512]{1,0:T(8,128)} async-done(((f32[32,512]{1,0:T(8,128)}), f32[32,512]{1,0:T(8,128)}) %all-reduce.5.cloned.1.call-update) | async-done | bytes 65552 | tf_op jit(solution)/shard_map/psum | solution.py:202
  1733.3 0.9 fusion.103
  1734.4 1.1 convolution_bitcast_fusion
  1735.5 1.1 add_select_fusion.18
  1736.6 1.1 copy.354
  1739.1 213.3 %reduce-scatter.5.cloned.1.call-done = f32[32,128]{1,0:T(8,128)} async-done(((f32[32,4096]{1,0:T(8,128)}), f32[32,128]{1,0:T(8,128)}) %reduce-scatter.5.cloned.1.call-update) | async-done | bytes 16400 | tf_op jit(solution)/shard_map/reduce_scatter | solution.py:204
  1952.4 0.7 fusion.343
  1953.7 135.7 %psum.46 = f32[2,2,32,32]{2,3,1,0:T(8,128)S(1)} all-reduce(f32[2,2,32,32]{2,3,1,0:T(8,128)S(1)} %pad_maximum_fusion.3), channel_id=1, replica_groups=mesh['row'=32,'col'=16] {'col'}, use_global_device_ids=true, to_apply=%region_10.12 | all-reduce | flops 4096 | bytes 32768 | tf_op jit(solution)/shard_map/psum | solution.py:210
  2089.4 197.0 %psum.47 = f32[2,2,32,32]{2,3,1,0:T(8,128)S(1)} all-reduce(f32[2,2,32,32]{2,3,1,0:T(8,128)S(1)} %psum.46), channel_id=1, replica_groups=mesh['row'=32,'col'=16] {'row'}, use_global_device_ids=true, to_apply=%region_11.13 | all-reduce | flops 4096 | bytes 32768 | tf_op jit(solution)/shard_map/psum | solution.py:210
  2286.5 403.5 %while.37 = (s32[]{:T(128)}, f32[32,64]{0,1:T(8,128)S(1)}, s32[]{:T(128)}, s32[]{:T(128)}, s32[]{:T(128)}, /*index=5*/s32[]{:T(128)}, s32[]{:T(128)}, f32[]{:T(128)}, f32[]{:T(128)}, f32[]{:T(128)}, /*index=10*/f32[]{:T(128)}) while((s32[]{:T(128)}, f32[32,64]{0,1:T(8,128)S(1)}, s32[]{:T(128)}, s32[]{:T(128)}, ...), condition=%wide.region_15.17_spmd.clone.clone, body=%wide.region_12.16_spmd.clone.clone.sunk | while | flops 87498 | bytes 50118 | solution.py:82
  (708 shorter events, 180.3 us)
Async XLA Ops:
  7.2 116.5 %copy-start = (s32[4,4,128,128]{3,2,1,0:T(8,128)S(1)}, s32[4,4,128,128]{3,2,1,0:T(8,128)}, u32[]{:S(2)}) copy-start(s32[4,4,128,128]{3,2,1,0:T(8,128)} %param.15) | copy-start | bytes 3145732
  7.2 369.3 %all-reduce.3.cloned.1.call-start = ((), (), s32[]{:S(2)}) async-start(), calls=%async_computation.2 | async-start | bytes 131072 | tf_op jit(solution)/shard_map/psum | solution.py:202
  125.7 0.7 copy-start.5
  125.7 0.8 copy-start.6
  125.7 470.4 %reduce-scatter.3.cloned.1.call-start = ((), (), s32[]{:S(2)}) async-start(), calls=%async_computation.3 | async-start | bytes 540672 | tf_op jit(solution)/shard_map/reduce_scatter | solution.py:204
  126.9 0.7 copy-start.7
  128.2 0.7 copy-start.8
  377.4 0.7 copy-start.4
  381.5 1351.8 %all-reduce.5.cloned.1.call-start = ((), (), s32[]{:S(2)}) async-start(), calls=%async_computation.4 | async-start | bytes 131072 | tf_op jit(solution)/shard_map/psum | solution.py:202
  382.0 0.7 copy-start.9
  382.0 0.7 copy-start.10
  382.8 0.7 copy-start.1
  1336.2 0.7 copy-start.2
  1439.2 513.2 %reduce-scatter.5.cloned.1.call-start = ((), (), s32[]{:S(2)}) async-start(), calls=%async_computation.5 | async-start | bytes 540672 | tf_op jit(solution)/shard_map/reduce_scatter | solution.py:204
  2691.5 0.7 copy-start.3
Sparse Core Ops, SparseCore 0:
  125.8 250.6 all-reduce.2
  381.6 214.5 reduce-scatter.2
  1439.3 293.9 all-reduce.4
  1737.9 214.5 reduce-scatter.4
